TPU v7x, 128 devices: a whole 4x4x4 slice. The times are simulated.
128 devices in a mesh: band: 16 (over x_hi, y, core), slab: 8 (over z, x_lo).
Axes of the slice: x: 4 (x_hi: 2, x_lo: 2; x = x_hi * 2 + x_lo), y: 4, z: 4, core: 2. Of those that a mesh axis runs over, the one named last changes fastest.
Arguments:
- orbitals: float32 [32, 72, 72, 72], P('band', 'slab'), may hold values from -5 to 5
- occupation: float32 [32], P('band'), may hold values from 0.3 to 1
Outputs:
- exchange_field: float32 [32, 72, 72, 72], P('band', 'slab')
All inputs are finite; a program needn't handle non-finite values.
Results may differ from a plain program's by a relative error of at most 0.0084.
Values may be sent and summed in bfloat16 or wider, within the bound.
A program may use at most 128 MiB of HBM per device.

v0:
```python
import math

import jax
import jax.numpy as jnp
import numpy as np
from jax import lax
from jax.experimental import pallas as pl
from jax.experimental.pallas import tpu as pltpu

N = 72
BOX_LENGTH = 37.25
ROWS, USED, LANES = 224, 216, 256
F32, BF16 = jnp.float32, jnp.bfloat16
MESH = pl.DeviceIdType.MESH
BLOCK = 24


def tables():
    positions = np.arange(N)
    angles = (positions[:, None] * positions[None, :] % N) * (2.0 * math.pi / N)
    cas = np.cos(angles) + np.sin(angles)
    spread = np.zeros((LANES, 384), np.float32)
    gather = np.zeros((384, LANES), np.float32)
    for part in range(3):
        spread[72 * part : 72 * part + 72, 128 * part : 128 * part + 72] = cas
        gather[128 * part : 128 * part + 72, 72 * part : 72 * part + 72] = cas
    squares = np.where(positions < N // 2, positions, positions - N).astype(np.float64) ** 2
    summed = squares[:, None, None] + squares[None, :, None] + squares[None, None, :]
    scale = 4.0 * math.pi / (2.0 * math.pi / BOX_LENGTH) ** 2 * (-1.0 / math.sqrt(32.0) / N**3)
    coulomb = np.zeros((N, N, 128), np.float32)
    coulomb[:, :, :N] = np.where(summed > 0, scale / np.where(summed > 0, summed, 1.0), 0.0)
    short = lambda value: jnp.asarray(value, F32).astype(BF16)
    return short(spread), short(cas), short(gather), jnp.asarray(coulomb)


class Place:
    def __init__(self):
        band, slab = lax.axis_index("band"), lax.axis_index("slab")
        xh, y, k = band // 8, band // 2 % 4, band % 2
        z, xl = slab // 2, slab % 2
        self.slab, self.z, self.y, self.k = slab, z, y, k
        group = xh * 4 + y
        w = (xh + xl) % 2
        column = w * 4 + z

        def swapped(of, against):
            return (of - against + 8) // 8

        kk = (k + swapped(group, column)) % 2
        far = group - column + 8
        self.diagonal = (far // 8) * ((16 - far) // 8)

        def member(xh2, xl2, y2):
            core = (kk + swapped(xh2 * 4 + y2, column)) % 2
            return (xh2 * 8 + y2 * 2 + core, 2 * z + xl2)

        self.row_x = (band, 2 * z + 1 - xl)
        self.row_ring = ((band, 2 * ((z + 1) % 4) + xl), (band, 2 * ((z + 3) % 4) + xl))
        self.col_x = member(1 - xh, 1 - xl, y)
        self.col_ring = (member(xh, xl, (y + 1) % 4), member(xh, xl, (y + 3) % 4))
        xh2 = (xh + xl + 1) % 2
        core = (k + swapped(xh2 * 4 + z, group)) % 2
        self.turn = (xh2 * 8 + z * 2 + core, 2 * y + 1 - xl)
        self.back = (w * 8 + z * 2 + kk, 2 * y + 1 - xl)
        self.row_slab = lambda step, line: 2 * ((z + step) % 4) + (1 - xl if line else xl)
        self.col_slab = lambda step, line: 2 * ((y + step) % 4) + (xl if line else 1 - xl)
        d = (y - z + 4) % 4
        half, last = d // 2, d // 3
        self.order = (half - last, 1 + 2 * half, 2 - 2 * half + last, 3 - half)

    def partners(self):
        return (self.row_x, *self.row_ring, self.col_x, *self.col_ring, self.turn, self.back)

    def pair(self, p):
        d, k = self.diagonal, self.k
        i = (1 - d) * (p // 2 if p < 4 else 0) + d * (0, 0, 1, 0, 1)[p]
        j = (1 - d) * (2 + p % 2) + d * ((0, 1, 1, 2, 3)[p] + (0, 0, 0, 1, -1)[p] * k)
        return i, j


def forward(orb, w, spread, cas, i, j, s, p):
    density = orb[i // 2, s, i % 2] * orb[j // 2, s, j % 2]
    h = jnp.dot(density, spread[...], preferred_element_type=F32)
    columns = [
        jnp.concatenate([h[24 * x : 24 * x + 24, 128 * t : 128 * t + 128] for t in range(3)], axis=0)
        for x in range(9)
    ]
    planes = jnp.dot(
        cas[...], jnp.concatenate(columns, axis=1).astype(BF16), preferred_element_type=F32
    )
    for x in range(9):
        w[p, pl.ds(pl.multiple_of(s * 648 + 72 * x, 8), 72), :] = planes[:, 128 * x : 128 * x + 128]


def middle(w, cas, coulomb, p, b):
    rows = [w[p, pl.ds(b + t, 72, stride=72), :] for t in range(BLOCK)]
    spectrum = jnp.dot(
        cas[...], jnp.concatenate(rows, axis=1).astype(BF16), preferred_element_type=F32
    )
    filtered = [spectrum[:, 128 * t : 128 * t + 128] * coulomb[b + t] for t in range(BLOCK)]
    back = jnp.dot(
        cas[...], jnp.concatenate(filtered, axis=1).astype(BF16), preferred_element_type=F32
    )
    for t in range(BLOCK):
        w[p, pl.ds(b + t, 72, stride=72), :] = back[:, 128 * t : 128 * t + 128]


def backward(orb, w, field, gather, cas, i, j, s, p):
    columns = [w[p, pl.ds(pl.multiple_of(s * 648 + 72 * x, 8), 72), :] for x in range(9)]
    half = jnp.dot(
        cas[...], jnp.concatenate(columns, axis=1).astype(BF16), preferred_element_type=F32
    )
    rows = [
        jnp.concatenate([half[24 * t : 24 * t + 24, 128 * x : 128 * x + 128] for t in range(3)], axis=1)
        for x in range(9)
    ]
    potential = jnp.dot(
        jnp.concatenate(rows, axis=0).astype(BF16), gather[...], preferred_element_type=F32
    )
    for target, source, weight in ((i, j, False), (j, i, True)):
        occupation = orb[source // 2, s, source % 2, 216:218].astype(F32)
        occupation = occupation[0:1] + occupation[1:2]
        if weight:
            occupation = occupation * jnp.where(i == j, 0.0, 1.0)
        term = (orb[source // 2, s, source % 2, 0:USED].astype(F32) * occupation) * potential
        field[target] = field[target] + term


def pack(value, occupation):
    parts = [
        jnp.concatenate([value[x, 24 * t : 24 * t + 24, :] for t in range(3)], axis=1) for x in range(9)
    ]
    body = jnp.concatenate(parts, axis=0)
    body = jnp.concatenate([body, jnp.zeros((USED, LANES - 216), F32)], axis=1)
    whole = jnp.full((8, LANES), occupation, F32)
    high = whole.astype(BF16).astype(F32)
    row = lax.broadcasted_iota(jnp.int32, (8, LANES), 0)
    tail = jnp.where(row == 0, high, jnp.where(row == 1, whole - high, 0.0))
    return jnp.concatenate([body, tail], axis=0).astype(BF16)


def kernel(
    mine, occupation, spread, cas, gather, coulomb_hbm, out,
    orb, w, field, part, land_half, land_ring, land_x, land_turn, coulomb, send_sem, recv_sem, copy_sem,
):
    me = Place()

    def remote(source, target, index, device):
        return pltpu.make_async_remote_copy(
            src_ref=source,
            dst_ref=target,
            send_sem=send_sem.at[index],
            recv_sem=recv_sem.at[index],
            device_id=device,
            device_id_type=MESH,
        )

    barrier = pltpu.get_barrier_semaphore()
    for device in me.partners():
        pl.semaphore_signal(barrier, inc=1, device_id=device, device_id_type=MESH)
    table = pltpu.make_async_copy(coulomb_hbm, coulomb, copy_sem)
    table.start()
    for o in range(2):
        orb[0, me.slab, o] = pack(mine[o], occupation[o])
    pl.semaphore_wait(barrier, len(me.partners()))

    sides = (
        (0, 0, me.row_slab, me.row_x, me.row_ring),
        (1, 9, me.col_slab, me.col_x, me.col_ring),
    )
    started = []

    def start(*copy):
        copy = remote(*copy)
        copy.start()
        started.append(copy)
        return copy

    def own(side):
        ab, base, slab, x, ring = side
        piece = orb.at[ab, slab(0, 0)]
        return [start(piece, piece, base + n, device) for n, device in enumerate((ring[0], ring[1], x))]

    def pass_x(side):
        ab, base, slab, _, ring = side
        piece = orb.at[ab, slab(0, 1)]
        return [start(piece, piece, base + 3 + n, ring[n]) for n in range(2)]

    def pass_half(side, line):
        ab, base, slab, _, ring = side
        pieces = [orb.at[ab, slab(3, line), 0], orb.at[ab, slab(1, line), 1]]
        return [start(pieces[n], pieces[n], base + 5 + 2 * line + n, ring[n]) for n in range(2)]

    row, col = sides
    origin = orb.at[0, me.slab]
    turned = start(origin, orb.at[1, me.slab], 18, me.turn)
    row_own = own(row)
    row_own[2].wait_recv()
    row_x = pass_x(row)
    turned.wait_recv()
    col_own = own(col)
    row_own[0].wait_recv()
    row_own[1].wait_recv()
    row_halves = pass_half(row, 0)
    col_own[2].wait_recv()
    col_x = pass_x(col)
    row_x[0].wait_recv()
    row_x[1].wait_recv()
    row_halves += pass_half(row, 1)
    col_own[0].wait_recv()
    col_own[1].wait_recv()
    col_halves = pass_half(col, 0)
    col_x[0].wait_recv()
    col_x[1].wait_recv()
    col_halves += pass_half(col, 1)

    def slab_of(first, t):
        step = me.order[first] + (me.order[first + 1] - me.order[first]) * (t // 2)
        return 2 * ((me.z + step) % 4) + t % 2

    def spectra(first):
        def body(t, _):
            s = slab_of(first, t)
            for p in range(4):
                i, j = me.pair(p)
                forward(orb, w, spread, cas, i, j, s, p)
            return 0

        lax.fori_loop(0, 4, body, 0)

    spectra(0)
    for copy in row_halves + col_halves:
        copy.wait_recv()
    spectra(2)

    @pl.when(me.diagonal == 1)
    def _():
        def body(s, _):
            i, j = me.pair(4)
            forward(orb, w, spread, cas, i, j, s, 4)
            return 0

        lax.fori_loop(0, 8, body, 0)

    table.wait()

    def solve(t, _):
        middle(w, cas, coulomb, t // (N // BLOCK), t % (N // BLOCK) * BLOCK)
        return 0

    lax.fori_loop(0, (4 + me.diagonal) * (N // BLOCK), solve, 0)

    def fields(first):
        def body(t, _):
            s = slab_of(first, t)
            field[...] = jnp.zeros_like(field)
            for p in range(4):
                i, j = me.pair(p)
                backward(orb, w, field, gather, cas, i, j, s, p)

            @pl.when(me.diagonal == 1)
            def _():
                i, j = me.pair(4)
                backward(orb, w, field, gather, cas, i, j, s, 4)

            for o in range(4):
                whole = jnp.concatenate([field[o], jnp.zeros((ROWS - USED, LANES), F32)], axis=0)
                part[o // 2, s, o % 2] = whole.astype(BF16)
            return 0

        lax.fori_loop(0, 4, body, 0)

    def add(*values):
        return sum((value.astype(F32) for value in values[1:]), values[0].astype(F32))

    fields(2)
    halves = {}
    for ab, base, slab, _, ring in sides:
        for line in (1, 0):
            for n in range(2):
                halves[ab, line, n] = start(
                    part.at[ab, slab(2, line), n],
                    land_half.at[ab, n, line],
                    19 + base + 2 * line + n,
                    ring[n],
                )
    fields(0)
    rings = {}
    for line in (1, 0):
        for n in range(2):
            for ab, base, slab, _, ring in sides:
                halves[ab, line, n].wait_recv()
                s = slab((1, 3)[n], line)
                part[ab, s, n] = add(part[ab, s, n], land_half[ab, n, line]).astype(BF16)
                rings[ab, line, n] = start(
                    part.at[ab, s], land_ring.at[ab, n, line], 23 + base + 2 * line + n, ring[n]
                )
    across = {}
    for ab, base, slab, x, _ in sides:
        rings[ab, 1, 0].wait_recv()
        rings[ab, 1, 1].wait_recv()
        s = slab(0, 1)
        part[ab, s] = add(part[ab, s], land_ring[ab, 0, 1], land_ring[ab, 1, 1]).astype(BF16)
        across[ab] = start(part.at[ab, s], land_x.at[ab], 27 + base, x)
    totals = {}
    for ab, base, slab, x, _ in (col, row):
        rings[ab, 0, 0].wait_recv()
        rings[ab, 0, 1].wait_recv()
        across[ab].wait_recv()
        s = slab(0, 0)
        part[ab, s] = add(
            part[ab, s], land_ring[ab, 0, 0], land_ring[ab, 1, 0], land_x[ab]
        ).astype(BF16)
        if ab == 1:
            turned_back = start(part.at[1, s], land_turn, 37, me.back)
    turned_back.wait_recv()
    s = me.row_slab(0, 0)
    for o in range(2):
        total = add(part[0, s, o], land_turn[o])
        for x in range(9):
            for t in range(3):
                out[o, x, 24 * t : 24 * t + 24, :] = total[24 * x : 24 * x + 24, 72 * t : 72 * t + 72]
    for copy in started:
        copy.wait_send()


def on_device(orbitals, occupation):
    vmem = pl.BlockSpec(memory_space=pltpu.VMEM)
    piece = (2, ROWS, LANES)
    return pl.pallas_call(
        kernel,
        out_shape=jax.ShapeDtypeStruct(orbitals.shape, F32),
        in_specs=[vmem, pl.BlockSpec(memory_space=pltpu.SMEM), vmem, vmem, vmem, pl.BlockSpec(memory_space=pl.ANY)],
        out_specs=vmem,
        scratch_shapes=[
            pltpu.VMEM((2, 8, *piece), BF16),
            pltpu.VMEM((5, N * N, 128), F32),
            pltpu.VMEM((4, USED, LANES), F32),
            pltpu.VMEM((2, 8, *piece), BF16),
            pltpu.VMEM((2, 2, 2, ROWS, LANES), BF16),
            pltpu.VMEM((2, 2, 2, *piece), BF16),
            pltpu.VMEM((2, *piece), BF16),
            pltpu.VMEM(piece, BF16),
            pltpu.VMEM((N, N, 128), F32),
            pltpu.SemaphoreType.DMA((38,)),
            pltpu.SemaphoreType.DMA((38,)),
            pltpu.SemaphoreType.DMA,
        ],
        compiler_params=pltpu.CompilerParams(
            collective_id=0, has_side_effects=True, vmem_limit_bytes=56 * 2**20
        ),
        name="exchange",
    )(orbitals, occupation, *tables())


def solution(mesh):
    return jax.shard_map(
        on_device,
        mesh=mesh,
        in_specs=(jax.sharding.PartitionSpec("band", "slab", None, None), jax.sharding.PartitionSpec("band")),
        out_specs=jax.sharding.PartitionSpec("band", "slab", None, None),
        check_vma=False,
    )
```

profile of v0, /device:TPU:25, one launch (start us, length us, event | category | flops | bytes accessed | tf_op | source)
XLA Modules:
  0.0 99.6 jit_solution(5708756587032292664)
XLA Ops:
  0.0 97.6 %exchange.1 = f32[2,9,72,72]{3,2,1,0:T(8,128)} custom-call(f32[2,9,72,72]{3,2,1,0:T(8,128)} %mine.1, f32[2]{0:T(128)} %occupation.1, bf16[256,384]{1,0:T(8,128)(2,1)} %constant.14.spread, bf16[72,72]{1,0:T(8,128)(2,1)} %constant.15.cas, bf16[384,256]{1,0:T(8,128)(2,1)} %constant.16.gather, f32[72,72,128]{2,1,0:T(8,128)} %constant.11.clone.coulomb_hbm), custom_call_target="tpu_custom_call" | custom-call | tf_op jit(solution)/shard_map/exchange/pallas_call | solution.py:330
  97.6 2.0 %copy.8 = f32[2,9,72,72]{3,2,1,0:T(8,128)} copy(f32[2,9,72,72]{3,2,1,0:T(8,128)} %exchange.1) | data formatting | bytes 746496
where the time goes:
time: 99.8 us; the launch traced here: 99.6 us
  Pallas kernels  97.6 us (98%)
  local copies, waits for them, and re-layouts  1.97 us (2%)
    pallas_call x1, Pallas kernels, on_device(): pl.pallas_call(kernel, out_shape=jax.ShapeDtypeStruct(orbitals.shape, F32...  97.6 us

commit v1 on v0

v1 whole, which is shorter than its diff:
```python
import math

import jax
import jax.numpy as jnp
import numpy as np
from jax import lax
from jax.experimental import pallas as pl
from jax.experimental.pallas import tpu as pltpu

N = 72
BOX_LENGTH = 37.25
ROWS, LANES, LINES = 96, 512, 648
F32, BF16 = jnp.float32, jnp.bfloat16
MESH = pl.DeviceIdType.MESH
BLOCK = 24


def tables():
    positions = np.arange(N)
    angles = (positions[:, None] * positions[None, :] % N) * (2.0 * math.pi / N)
    cas = np.cos(angles) + np.sin(angles)
    spread = np.zeros((4, 256, 256), np.float32)
    gather = np.zeros((4, 256, 256), np.float32)
    for block in range(7):
        window, lane = block // 2, 72 * block - 128 * (block // 2)
        column = 128 * (block % 2)
        spread[window, lane : lane + 72, column : column + 72] = cas
        gather[window, column : column + 72, lane : lane + 72] = cas
    squares = np.where(positions < N // 2, positions, positions - N).astype(np.float64) ** 2
    summed = squares[:, None, None] + squares[None, :, None] + squares[None, None, :]
    scale = 4.0 * math.pi / (2.0 * math.pi / BOX_LENGTH) ** 2 * (-1.0 / math.sqrt(32.0) / N**3)
    coulomb = np.zeros((N, N, 128), np.float32)
    coulomb[:, :, :N] = np.where(summed > 0, scale / np.where(summed > 0, summed, 1.0), 0.0)
    short = lambda value: jnp.asarray(value, F32).astype(BF16)
    return short(spread), short(cas), short(gather), jnp.asarray(coulomb)


class Place:
    def __init__(self):
        band, slab = lax.axis_index("band"), lax.axis_index("slab")
        xh, y, k = band // 8, band // 2 % 4, band % 2
        z, xl = slab // 2, slab % 2
        self.slab, self.z, self.y, self.k = slab, z, y, k
        group = xh * 4 + y
        w = (xh + xl) % 2
        column = w * 4 + z

        def swapped(of, against):
            return (of - against + 8) // 8

        kk = (k + swapped(group, column)) % 2
        far = group - column + 8
        self.diagonal = (far // 8) * ((16 - far) // 8)

        def member(xh2, xl2, y2):
            core = (kk + swapped(xh2 * 4 + y2, column)) % 2
            return (xh2 * 8 + y2 * 2 + core, 2 * z + xl2)

        self.row_x = (band, 2 * z + 1 - xl)
        self.row_ring = ((band, 2 * ((z + 1) % 4) + xl), (band, 2 * ((z + 3) % 4) + xl))
        self.col_x = member(1 - xh, 1 - xl, y)
        self.col_ring = (member(xh, xl, (y + 1) % 4), member(xh, xl, (y + 3) % 4))
        xh2 = (xh + xl + 1) % 2
        y2 = (2 * y - z + 4) % 4
        core = (k + swapped(xh2 * 4 + y2, group)) % 2
        self.turn = (xh2 * 8 + y2 * 2 + core, 2 * y + 1 - xl)
        self.back = (w * 8 + z * 2 + kk, 2 * ((2 * z - y + 4) % 4) + 1 - xl)
        self.row_slab = lambda step, line: 2 * ((z + step) % 4) + (1 - xl if line else xl)
        self.col_slab = lambda step, line: 2 * ((2 * z - y - step + 8) % 4) + (xl if line else 1 - xl)
        d = (z - y + 4) % 4
        half, last, some = d // 2, d // 3, (d + 2) // 3
        self.way_in = (half - last, 1 + 2 * half, 2 - 2 * half + last, 3 - half)
        self.way_out = ((d + 2) % 4, 1 + some, 3 - 3 * some + half - last, d + half - last)

    def partners(self):
        return (self.row_x, *self.row_ring, self.col_x, *self.col_ring, self.turn, self.back)

    def pair(self, p):
        d, k = self.diagonal, self.k
        i = (1 - d) * (p // 2 if p < 4 else 0) + d * (0, 0, 1, 0, 1)[p]
        j = (1 - d) * (2 + p % 2) + d * ((0, 1, 1, 2, 3)[p] + (0, 0, 0, 1, -1)[p] * k)
        return i, j


def lines_of(blocks, first, count):
    pieces = []
    while count:
        block, row = first // ROWS, first % ROWS
        size = min(count, ROWS - row)
        pieces.append(blocks[block][row : row + size])
        first, count = first + size, count - size
    return pieces[0] if len(pieces) == 1 else jnp.concatenate(pieces, axis=0)


def forward(orb, w, spread, cas, i, j, s, p):
    density = orb[i // 2, s, i % 2] * orb[j // 2, s, j % 2]
    blocks = []
    for t in range(3):
        h = jnp.dot(density[:, 128 * t : 128 * t + 256], spread[t], preferred_element_type=F32)
        blocks += [h[:, 0:128], h[:, 128:256]]
    blocks.append(jnp.dot(density[:, 384:512], spread[3, 0:128, 0:128], preferred_element_type=F32))
    columns = [lines_of(blocks, 72 * x, 72) for x in range(9)]
    planes = jnp.dot(
        cas[...], jnp.concatenate(columns, axis=1).astype(BF16), preferred_element_type=F32
    )
    for x in range(9):
        w[p, pl.ds(pl.multiple_of(s * LINES + 72 * x, 8), 72), :] = planes[:, 128 * x : 128 * x + 128]


def middle(w, cas, coulomb, p, b):
    rows = [w[p, pl.ds(b + t, 72, stride=72), :] for t in range(BLOCK)]
    spectrum = jnp.dot(
        cas[...], jnp.concatenate(rows, axis=1).astype(BF16), preferred_element_type=F32
    )
    filtered = [spectrum[:, 128 * t : 128 * t + 128] * coulomb[b + t] for t in range(BLOCK)]
    back = jnp.dot(
        cas[...], jnp.concatenate(filtered, axis=1).astype(BF16), preferred_element_type=F32
    )
    for t in range(BLOCK):
        w[p, pl.ds(b + t, 72, stride=72), :] = back[:, 128 * t : 128 * t + 128]


def backward(orb, w, field, gather, cas, occupied, i, j, s, p):
    columns = [w[p, pl.ds(pl.multiple_of(s * LINES + 72 * x, 8), 72), :] for x in range(9)]
    half = jnp.dot(
        cas[...], jnp.concatenate(columns, axis=1).astype(BF16), preferred_element_type=F32
    )
    lines = jnp.concatenate([half[:, 128 * x : 128 * x + 128] for x in range(9)], axis=0).astype(BF16)
    rows = [lines[ROWS * t : min(ROWS * t + ROWS, LINES)] for t in range(7)]
    parts = []
    for t in range(3):
        h = jnp.dot(
            jnp.concatenate(rows[2 * t : 2 * t + 2], axis=1), gather[t], preferred_element_type=F32
        )
        parts.append((h[:, 0:128], h[:, 128:256]))
    h = jnp.dot(rows[6], gather[3, 0:128, 0:128], preferred_element_type=F32)
    h = jnp.concatenate([h, jnp.zeros((7 * ROWS - LINES, 128), F32)], axis=0)
    potential = jnp.concatenate(
        [parts[0][0], parts[0][1] + parts[1][0], parts[1][1] + parts[2][0], parts[2][1] + h], axis=1
    )
    for target, source, other in ((i, j, False), (j, i, True)):
        weight = occupied[source, 0:1, :]
        if other:
            weight = weight * jnp.where(i == j, 0.0, 1.0)
        field[target] += (orb[source // 2, s, source % 2].astype(F32) * weight) * potential


def pack(value, occupation):
    lines = jnp.concatenate([value[x] for x in range(9)], axis=0)
    blocks = [lines[ROWS * t : ROWS * t + ROWS] for t in range(6)]
    blocks.append(jnp.concatenate([lines[6 * ROWS :], jnp.zeros((7 * ROWS - LINES, N), F32)], axis=0))
    whole = jnp.full((ROWS, LANES - 7 * N), occupation, F32)
    high = whole.astype(BF16).astype(F32)
    lane = lax.broadcasted_iota(jnp.int32, whole.shape, 1)
    blocks.append(jnp.where(lane == 0, high, jnp.where(lane == 1, whole - high, 0.0)))
    return jnp.concatenate(blocks, axis=1).astype(BF16)


def kernel(
    mine, occupation, spread, cas, gather, coulomb_hbm, out,
    orb, w, field, part, land_half, land_ring, land_x, land_turn, coulomb, occupied, send_sem, recv_sem, copy_sem,
):
    me = Place()
    started = []

    def start(source, target, index, device):
        copy = pltpu.make_async_remote_copy(
            src_ref=source,
            dst_ref=target,
            send_sem=send_sem.at[index],
            recv_sem=recv_sem.at[index],
            device_id=device,
            device_id_type=MESH,
        )
        copy.start()
        started.append(copy)
        return copy

    barrier = pltpu.get_barrier_semaphore()
    for device in me.partners():
        pl.semaphore_signal(barrier, inc=1, device_id=device, device_id_type=MESH)
    table = pltpu.make_async_copy(coulomb_hbm, coulomb, copy_sem)
    table.start()
    for o in range(2):
        orb[0, me.slab, o] = pack(mine[o], occupation[o])
    pl.semaphore_wait(barrier, len(me.partners()))

    row = (0, 0, me.row_slab, me.row_x, me.row_ring)
    col = (1, 14, me.col_slab, me.col_x, me.col_ring)
    sides = (col, row)

    def own(side, o):
        ab, base, slab, x, ring = side
        piece = orb.at[ab, slab(0, 0), o]
        return [start(piece, piece, base + 3 * o + n, device) for n, device in enumerate((x, *ring))]

    def pass_x(side, o):
        ab, base, slab, _, ring = side
        piece = orb.at[ab, slab(0, 1), o]
        return [start(piece, piece, base + 6 + 2 * o + n, ring[n]) for n in range(2)]

    def pass_far(side, line, n):
        ab, base, slab, _, ring = side
        piece = orb.at[ab, slab((3, 1)[n], line), n]
        return start(piece, piece, base + 10 + 2 * line + n, ring[n])

    turned = [start(orb.at[0, me.slab, o], orb.at[1, me.slab, o], 28 + o, me.turn) for o in range(2)]
    row_own = [own(row, o) for o in range(2)]
    row_x, col_x, col_own, far = [], [], [], []
    for o in range(2):
        row_own[o][0].wait_recv()
        row_x.append(pass_x(row, o))
    turned[0].wait_recv()
    col_own.append(own(col, 0))
    row_own[0][1].wait_recv()
    far.append(pass_far(row, 0, 0))
    turned[1].wait_recv()
    col_own.append(own(col, 1))
    row_own[1][2].wait_recv()
    far.append(pass_far(row, 0, 1))
    for o in range(2):
        col_own[o][0].wait_recv()
        col_x.append(pass_x(col, o))
    for n in range(2):
        row_x[n][n].wait_recv()
        far.append(pass_far(row, 1, n))
    for n in range(2):
        col_own[n][1 + n].wait_recv()
        far.append(pass_far(col, 0, n))
    for n in range(2):
        col_x[n][n].wait_recv()
        far.append(pass_far(col, 1, n))
    for n in range(2):
        row_own[n][2 - n].wait_recv()
        row_x[n][1 - n].wait_recv()
        col_own[n][2 - n].wait_recv()
        col_x[n][1 - n].wait_recv()

    def slab_at(steps, t):
        step = steps[0]
        for n in range(1, len(steps)):
            reached = (t // 2 + 4 - n) // 4
            step = step + (steps[n] - steps[n - 1]) * reached
        return 2 * ((me.z + step) % 4) + t % 2

    def spectra(pairs, steps):
        def body(t, _):
            s = slab_at(steps, t)
            for p in pairs:
                i, j = me.pair(p)
                forward(orb, w, spread, cas, i, j, s, p)
            return 0

        lax.fori_loop(0, 2 * len(steps), body, 0)

    on_diagonal = me.diagonal == 1
    off_diagonal = me.diagonal == 0
    pl.when(off_diagonal)(lambda: spectra(range(4), me.way_in[0:2]))
    for copy in far[:4]:
        copy.wait_recv()
    pl.when(on_diagonal)(lambda: spectra(range(3), me.way_in))
    for copy in far[4:]:
        copy.wait_recv()
    pl.when(off_diagonal)(lambda: spectra(range(4), me.way_in[2:4]))
    pl.when(on_diagonal)(lambda: spectra(range(3, 5), me.way_in))

    for q in range(4):
        terms = orb[q // 2, me.slab, q % 2, 0:16, 384:512].astype(F32)[0:8]
        occupied[q] = jnp.broadcast_to(terms[:, 120:121] + terms[:, 121:122], (8, LANES))
    table.wait()

    def solve(t, _):
        middle(w, cas, coulomb, t // (N // BLOCK), t % (N // BLOCK) * BLOCK)
        return 0

    lax.fori_loop(0, (4 + me.diagonal) * (N // BLOCK), solve, 0)

    def fields(steps):
        def body(t, _):
            s = slab_at(steps, t)
            field[...] = jnp.zeros_like(field)

            def pairs(count):
                for p in range(count):
                    i, j = me.pair(p)
                    backward(orb, w, field, gather, cas, occupied, i, j, s, p)

            pl.when(off_diagonal)(lambda: pairs(4))
            pl.when(on_diagonal)(lambda: pairs(5))
            for o in range(4):
                part[o // 2, s, o % 2] = field[o].astype(BF16)
            return 0

        lax.fori_loop(0, 2 * len(steps), body, 0)

    def add(*values):
        return sum((value.astype(F32) for value in values[1:]), values[0].astype(F32))

    far = {}

    def send_far(side):
        ab, base, slab, _, ring = side
        for line in (1, 0):
            for n in range(2):
                source = part.at[ab, slab(2, line), n]
                far[ab, line, n] = start(source, land_half.at[ab, n, line], 30 + base + 2 * line + n, ring[n])

    near = {}

    def send_near(side, line, o, n):
        ab, base, slab, _, ring = side
        s = slab((1, 3)[n], line)
        if o == n:
            far[ab, line, n].wait_recv()
            part[ab, s, o] = add(part[ab, s, o], land_half[ab, n, line]).astype(BF16)
        index = 34 + base + 4 * line + 2 * o + n
        near[ab, line, o, n] = start(part.at[ab, s, o], land_ring.at[ab, n, line, o], index, ring[n])

    across = {}

    def send_across(side, o):
        ab, base, slab, x, _ = side
        s = slab(0, 1)
        for n in range(2):
            near[ab, 1, o, n].wait_recv()
        part[ab, s, o] = add(part[ab, s, o], land_ring[ab, 0, 1, o], land_ring[ab, 1, 1, o]).astype(BF16)
        across[ab, o] = start(part.at[ab, s, o], land_x.at[ab, o], 42 + base + o, x)

    def total(side, o):
        ab, _, slab, _, _ = side
        for n in range(2):
            near[ab, 0, o, n].wait_recv()
        across[ab, o].wait_recv()
        return add(part[ab, slab(0, 0), o], land_ring[ab, 0, 0, o], land_ring[ab, 1, 0, o], land_x[ab, o])

    fields(me.way_out[0:1])
    send_far(col)
    fields(me.way_out[1:2])
    send_far(row)
    fields(me.way_out[2:4])
    for line in (1, 0):
        for o in range(2):
            for side in sides:
                send_near(side, line, o, 1 - o)
        for o in range(2):
            for side in sides:
                send_near(side, line, o, o)
    for o in range(2):
        for side in sides:
            send_across(side, o)
    returned = []
    for o in range(2):
        part[1, me.col_slab(0, 0), o] = total(col, o).astype(BF16)
        returned.append(start(part.at[1, me.col_slab(0, 0), o], land_turn.at[o], 58 + o, me.back))
    for o in range(2):
        field[o] = total(row, o)
    for o in range(2):
        returned[o].wait_recv()
        whole = field[o] + land_turn[o].astype(F32)
        blocks = [whole[:, 72 * t : 72 * t + 72] for t in range(7)]
        for x in range(9):
            out[o, x] = lines_of(blocks, 72 * x, 72)
    for copy in started:
        copy.wait_send()


def on_device(orbitals, occupation):
    vmem = pl.BlockSpec(memory_space=pltpu.VMEM)
    piece = (ROWS, LANES)
    return pl.pallas_call(
        kernel,
        out_shape=jax.ShapeDtypeStruct(orbitals.shape, F32),
        in_specs=[vmem, pl.BlockSpec(memory_space=pltpu.SMEM), vmem, vmem, vmem, pl.BlockSpec(memory_space=pl.ANY)],
        out_specs=vmem,
        scratch_shapes=[
            pltpu.VMEM((2, 8, 2, *piece), BF16),
            pltpu.VMEM((5, N * N, 128), F32),
            pltpu.VMEM((4, *piece), F32),
            pltpu.VMEM((2, 8, 2, *piece), BF16),
            pltpu.VMEM((2, 2, 2, *piece), BF16),
            pltpu.VMEM((2, 2, 2, 2, *piece), BF16),
            pltpu.VMEM((2, 2, *piece), BF16),
            pltpu.VMEM((2, *piece), BF16),
            pltpu.VMEM((N, N, 128), F32),
            pltpu.VMEM((4, 8, LANES), F32),
            pltpu.SemaphoreType.DMA((60,)),
            pltpu.SemaphoreType.DMA((60,)),
            pltpu.SemaphoreType.DMA,
        ],
        compiler_params=pltpu.CompilerParams(
            collective_id=0, has_side_effects=True, vmem_limit_bytes=56 * 2**20
        ),
        name="exchange",
    )(orbitals, occupation, *tables())


def solution(mesh):
    return jax.shard_map(
        on_device,
        mesh=mesh,
        in_specs=(jax.sharding.PartitionSpec("band", "slab", None, None), jax.sharding.PartitionSpec("band")),
        out_specs=jax.sharding.PartitionSpec("band", "slab", None, None),
        check_vma=False,
    )
```

time: 99.8 us -> 81.4 us (0.82)
  the two profiles are of different devices: /device:TPU:25 before, /device:TPU:35 now
where the time goes in v1:
time: 81.4 us; the launch traced here: 81.2 us
  Pallas kernels  79.2 us (97%)
  local copies, waits for them, and re-layouts  1.97 us (2%)
    pallas_call x1, Pallas kernels, on_device(): pl.pallas_call(kernel, out_shape=jax.ShapeDtypeStruct(orbitals.shape, F32...  79.2 us
    unnamed x1, local copies, waits for them, and re-layouts  1.97 us

profile of v1, /device:TPU:35, one launch (start us, length us, event | category | flops | bytes accessed | tf_op | source)
XLA Modules:
  0.0 81.2 jit_solution(850721512397378190)
XLA Ops:
  0.0 79.2 %exchange.1 = f32[2,9,72,72]{3,2,1,0:T(8,128)} custom-call(f32[2,9,72,72]{3,2,1,0:T(8,128)} %mine.1, f32[2]{0:T(128)} %occupation.1, bf16[4,256,256]{2,1,0:T(8,128)(2,1)} %constant.14.spread, bf16[72,72]{1,0:T(8,128)(2,1)} %constant.15.cas, bf16[4,256,256]{2,1,0:T(8,128)(2,1)} %constant.16.gather, f32[72,72,128]{2,1,0:T(8,128)} %constant.11.clone.coulomb_hbm), custom_call_target="tpu_custom_call" | custom-call | tf_op jit(solution)/shard_map/exchange/pallas_call | solution.py:370
  79.2 2.0 %copy.8 = f32[2,9,72,72]{3,2,1,0:T(8,128)} copy(f32[2,9,72,72]{3,2,1,0:T(8,128)} %exchange.1) | data formatting | bytes 746496

commit v2 on v1

--- a/solution.py
+++ b/solution.py
@@ -12,7 +12,7 @@
 ROWS, LANES, LINES = 96, 512, 648
 F32, BF16 = jnp.float32, jnp.bfloat16
 MESH = pl.DeviceIdType.MESH
-BLOCK = 24
+BLOCK = 36
 
 
 def tables():
@@ -75,12 +75,6 @@
     def partners(self):
         return (self.row_x, *self.row_ring, self.col_x, *self.col_ring, self.turn, self.back)
 
-    def pair(self, p):
-        d, k = self.diagonal, self.k
-        i = (1 - d) * (p // 2 if p < 4 else 0) + d * (0, 0, 1, 0, 1)[p]
-        j = (1 - d) * (2 + p % 2) + d * ((0, 1, 1, 2, 3)[p] + (0, 0, 0, 1, -1)[p] * k)
-        return i, j
-
 
 def lines_of(blocks, first, count):
     pieces = []
@@ -92,19 +86,25 @@
     return pieces[0] if len(pieces) == 1 else jnp.concatenate(pieces, axis=0)
 
 
-def forward(orb, w, spread, cas, i, j, s, p):
-    density = orb[i // 2, s, i % 2] * orb[j // 2, s, j % 2]
-    blocks = []
-    for t in range(3):
-        h = jnp.dot(density[:, 128 * t : 128 * t + 256], spread[t], preferred_element_type=F32)
-        blocks += [h[:, 0:128], h[:, 128:256]]
-    blocks.append(jnp.dot(density[:, 384:512], spread[3, 0:128, 0:128], preferred_element_type=F32))
-    columns = [lines_of(blocks, 72 * x, 72) for x in range(9)]
-    planes = jnp.dot(
-        cas[...], jnp.concatenate(columns, axis=1).astype(BF16), preferred_element_type=F32
-    )
-    for x in range(9):
-        w[p, pl.ds(pl.multiple_of(s * LINES + 72 * x, 8), 72), :] = planes[:, 128 * x : 128 * x + 128]
+def forward(orb, w, spread, cas, units):
+    densities = [orb[i // 2, s, i % 2] * orb[j // 2, s, j % 2] for i, j, s, _ in units]
+
+    def stacked(first, last, table):
+        rows = jnp.concatenate([density[:, first:last] for density in densities], axis=0)
+        return jnp.dot(rows, table, preferred_element_type=F32)
+
+    windows = [stacked(128 * t, 128 * t + 256, spread[t]) for t in range(3)]
+    last = stacked(384, 512, spread[3, 0:128, 0:128])
+    for n, (_, _, s, p) in enumerate(units):
+        rows = slice(ROWS * n, ROWS * n + ROWS)
+        blocks = [window[rows, 128 * t : 128 * t + 128] for window in windows for t in range(2)]
+        blocks.append(last[rows])
+        columns = [lines_of(blocks, 72 * x, 72) for x in range(9)]
+        planes = jnp.dot(
+            cas[...], jnp.concatenate(columns, axis=1).astype(BF16), preferred_element_type=F32
+        )
+        for x in range(9):
+            w[p, pl.ds(pl.multiple_of(s * LINES + 72 * x, 8), 72), :] = planes[:, 128 * x : 128 * x + 128]
 
 
 def middle(w, cas, coulomb, p, b):
@@ -120,29 +120,37 @@
         w[p, pl.ds(b + t, 72, stride=72), :] = back[:, 128 * t : 128 * t + 128]
 
 
-def backward(orb, w, field, gather, cas, occupied, i, j, s, p):
-    columns = [w[p, pl.ds(pl.multiple_of(s * LINES + 72 * x, 8), 72), :] for x in range(9)]
-    half = jnp.dot(
-        cas[...], jnp.concatenate(columns, axis=1).astype(BF16), preferred_element_type=F32
-    )
-    lines = jnp.concatenate([half[:, 128 * x : 128 * x + 128] for x in range(9)], axis=0).astype(BF16)
-    rows = [lines[ROWS * t : min(ROWS * t + ROWS, LINES)] for t in range(7)]
-    parts = []
+def backward(w, gather, cas, units):
+    lines = []
+    for s, p in units:
+        columns = [w[p, pl.ds(pl.multiple_of(s * LINES + 72 * x, 8), 72), :] for x in range(9)]
+        half = jnp.dot(
+            cas[...], jnp.concatenate(columns, axis=1).astype(BF16), preferred_element_type=F32
+        )
+        rows = [half[:, 128 * x : 128 * x + 128] for x in range(9)]
+        rows.append(jnp.zeros((7 * ROWS - LINES, 128), F32))
+        lines.append(jnp.concatenate(rows, axis=0).astype(BF16))
+    windows = []
     for t in range(3):
-        h = jnp.dot(
-            jnp.concatenate(rows[2 * t : 2 * t + 2], axis=1), gather[t], preferred_element_type=F32
+        first = 2 * t * ROWS
+        rows = [
+            jnp.concatenate([line[first : first + ROWS], line[first + ROWS : first + 2 * ROWS]], axis=1)
+            for line in lines
+        ]
+        windows.append(jnp.dot(jnp.concatenate(rows, axis=0), gather[t], preferred_element_type=F32))
+    rows = jnp.concatenate([line[6 * ROWS :] for line in lines], axis=0)
+    last = jnp.dot(rows, gather[3, 0:128, 0:128], preferred_element_type=F32)
+    potentials = []
+    for n in range(len(units)):
+        rows = slice(ROWS * n, ROWS * n + ROWS)
+        a, b, c = (window[rows] for window in windows)
+        potentials.append(
+            jnp.concatenate(
+                [a[:, 0:128], a[:, 128:] + b[:, 0:128], b[:, 128:] + c[:, 0:128], c[:, 128:] + last[rows]],
+                axis=1,
+            )
         )
-        parts.append((h[:, 0:128], h[:, 128:256]))
-    h = jnp.dot(rows[6], gather[3, 0:128, 0:128], preferred_element_type=F32)
-    h = jnp.concatenate([h, jnp.zeros((7 * ROWS - LINES, 128), F32)], axis=0)
-    potential = jnp.concatenate(
-        [parts[0][0], parts[0][1] + parts[1][0], parts[1][1] + parts[2][0], parts[2][1] + h], axis=1
-    )
-    for target, source, other in ((i, j, False), (j, i, True)):
-        weight = occupied[source, 0:1, :]
-        if other:
-            weight = weight * jnp.where(i == j, 0.0, 1.0)
-        field[target] += (orb[source // 2, s, source % 2].astype(F32) * weight) * potential
+    return potentials
 
 
 def pack(value, occupation):
@@ -158,7 +166,7 @@
 
 def kernel(
     mine, occupation, spread, cas, gather, coulomb_hbm, out,
-    orb, w, field, part, land_half, land_ring, land_x, land_turn, coulomb, occupied, send_sem, recv_sem, copy_sem,
+    orb, w, acc, part, land_half, land_ring, land_x, land_turn, coulomb, occupied, send_sem, recv_sem, copy_sem,
 ):
     me = Place()
     started = []
@@ -206,117 +214,100 @@
 
     turned = [start(orb.at[0, me.slab, o], orb.at[1, me.slab, o], 28 + o, me.turn) for o in range(2)]
     row_own = [own(row, o) for o in range(2)]
-    row_x, col_x, col_own, far = [], [], [], []
+    row_x, col_x, col_own, row_far, col_far = [], [], [], [], [[], []]
     for o in range(2):
         row_own[o][0].wait_recv()
         row_x.append(pass_x(row, o))
     turned[0].wait_recv()
     col_own.append(own(col, 0))
     row_own[0][1].wait_recv()
-    far.append(pass_far(row, 0, 0))
+    row_far.append(pass_far(row, 0, 0))
     turned[1].wait_recv()
     col_own.append(own(col, 1))
     row_own[1][2].wait_recv()
-    far.append(pass_far(row, 0, 1))
-    for o in range(2):
-        col_own[o][0].wait_recv()
-        col_x.append(pass_x(col, o))
+    row_far.append(pass_far(row, 0, 1))
+    col_own[0][0].wait_recv()
+    col_x.append(pass_x(col, 0))
+    col_own[0][1].wait_recv()
+    col_far[0].append(pass_far(col, 0, 0))
     for n in range(2):
         row_x[n][n].wait_recv()
-        far.append(pass_far(row, 1, n))
-    for n in range(2):
-        col_own[n][1 + n].wait_recv()
-        far.append(pass_far(col, 0, n))
-    for n in range(2):
-        col_x[n][n].wait_recv()
-        far.append(pass_far(col, 1, n))
+        row_far.append(pass_far(row, 1, n))
+    col_own[1][0].wait_recv()
+    col_x.append(pass_x(col, 1))
+    col_x[0][0].wait_recv()
+    col_far[0].append(pass_far(col, 1, 0))
+    col_own[1][2].wait_recv()
+    col_far[1].append(pass_far(col, 0, 1))
     for n in range(2):
         row_own[n][2 - n].wait_recv()
         row_x[n][1 - n].wait_recv()
-        col_own[n][2 - n].wait_recv()
-        col_x[n][1 - n].wait_recv()
-
-    def slab_at(steps, t):
+    col_own[0][2].wait_recv()
+    col_x[0][1].wait_recv()
+
+    k, d = me.k, me.diagonal
+    on_diagonal, off_diagonal = d == 1, d == 0
+
+    def step_at(steps, t):
         step = steps[0]
         for n in range(1, len(steps)):
-            reached = (t // 2 + 4 - n) // 4
-            step = step + (steps[n] - steps[n - 1]) * reached
-        return 2 * ((me.z + step) % 4) + t % 2
-
-    def spectra(pairs, steps):
+            step = step + (steps[n] - steps[n - 1]) * ((t + len(steps) - n) // len(steps))
+        return step
+
+    def slabs_at(step):
+        return [2 * ((me.z + step) % 4) + line for line in range(2)]
+
+    def over(steps, group, body):
+        firsts = [steps[n::group] for n in range(group)]
+
+        def run(t, _):
+            body([slab for own_steps in firsts for slab in slabs_at(step_at(own_steps, t))])
+            return 0
+
+        lax.fori_loop(0, len(steps) // group, run, 0)
+
+    def spectra(pairs, steps, group=1):
+        over(
+            steps,
+            group,
+            lambda slabs: forward(
+                orb, w, spread, cas, [(i, j, s, p) for s in slabs for p, (i, j) in pairs]
+            ),
+        )
+
+    def solve(count):
         def body(t, _):
-            s = slab_at(steps, t)
-            for p in pairs:
-                i, j = me.pair(p)
-                forward(orb, w, spread, cas, i, j, s, p)
+            middle(w, cas, coulomb, t // (N // BLOCK), t % (N // BLOCK) * BLOCK)
             return 0
 
-        lax.fori_loop(0, 2 * len(steps), body, 0)
-
-    on_diagonal = me.diagonal == 1
-    off_diagonal = me.diagonal == 0
-    pl.when(off_diagonal)(lambda: spectra(range(4), me.way_in[0:2]))
-    for copy in far[:4]:
-        copy.wait_recv()
-    pl.when(on_diagonal)(lambda: spectra(range(3), me.way_in))
-    for copy in far[4:]:
-        copy.wait_recv()
-    pl.when(off_diagonal)(lambda: spectra(range(4), me.way_in[2:4]))
-    pl.when(on_diagonal)(lambda: spectra(range(3, 5), me.way_in))
-
-    for q in range(4):
-        terms = orb[q // 2, me.slab, q % 2, 0:16, 384:512].astype(F32)[0:8]
-        occupied[q] = jnp.broadcast_to(terms[:, 120:121] + terms[:, 121:122], (8, LANES))
-    table.wait()
-
-    def solve(t, _):
-        middle(w, cas, coulomb, t // (N // BLOCK), t % (N // BLOCK) * BLOCK)
-        return 0
-
-    lax.fori_loop(0, (4 + me.diagonal) * (N // BLOCK), solve, 0)
-
-    def fields(steps):
-        def body(t, _):
-            s = slab_at(steps, t)
-            field[...] = jnp.zeros_like(field)
-
-            def pairs(count):
-                for p in range(count):
-                    i, j = me.pair(p)
-                    backward(orb, w, field, gather, cas, occupied, i, j, s, p)
-
-            pl.when(off_diagonal)(lambda: pairs(4))
-            pl.when(on_diagonal)(lambda: pairs(5))
-            for o in range(4):
-                part[o // 2, s, o % 2] = field[o].astype(BF16)
-            return 0
-
-        lax.fori_loop(0, 2 * len(steps), body, 0)
+        lax.fori_loop(0, count * (N // BLOCK), body, 0)
+
+    def weighed(q, s, factor=None):
+        weight = occupied[q, 0:1, :]
+        if factor is not None:
+            weight = weight * factor
+        return orb[q // 2, s, q % 2].astype(F32) * weight
 
     def add(*values):
         return sum((value.astype(F32) for value in values[1:]), values[0].astype(F32))
 
-    far = {}
-
-    def send_far(side):
+    far, near, across, returned = {}, {}, {}, {}
+
+    def send_far(side, o):
         ab, base, slab, _, ring = side
         for line in (1, 0):
-            for n in range(2):
-                source = part.at[ab, slab(2, line), n]
-                far[ab, line, n] = start(source, land_half.at[ab, n, line], 30 + base + 2 * line + n, ring[n])
-
-    near = {}
-
-    def send_near(side, line, o, n):
+            source = part.at[ab, slab(2, line), o]
+            far[ab, line, o] = start(source, land_half.at[ab, o, line], 30 + base + 2 * line + o, ring[o])
+
+    def send_near(side, o, n):
         ab, base, slab, _, ring = side
-        s = slab((1, 3)[n], line)
-        if o == n:
-            far[ab, line, n].wait_recv()
-            part[ab, s, o] = add(part[ab, s, o], land_half[ab, n, line]).astype(BF16)
-        index = 34 + base + 4 * line + 2 * o + n
-        near[ab, line, o, n] = start(part.at[ab, s, o], land_ring.at[ab, n, line, o], index, ring[n])
-
-    across = {}
+        for line in (1, 0):
+            s = slab((1, 3)[n], line)
+            if o == n:
+                far[ab, line, n].wait_recv()
+                part[ab, s, o] = add(part[ab, s, o], land_half[ab, n, line]).astype(BF16)
+            index = 34 + base + 4 * line + 2 * o + n
+            near[ab, line, o, n] = start(part.at[ab, s, o], land_ring.at[ab, n, line, o], index, ring[n])
 
     def send_across(side, o):
         ab, base, slab, x, _ = side
@@ -333,30 +324,108 @@
         across[ab, o].wait_recv()
         return add(part[ab, slab(0, 0), o], land_ring[ab, 0, 0, o], land_ring[ab, 1, 0, o], land_x[ab, o])
 
-    fields(me.way_out[0:1])
-    send_far(col)
-    fields(me.way_out[1:2])
-    send_far(row)
-    fields(me.way_out[2:4])
-    for line in (1, 0):
-        for o in range(2):
-            for side in sides:
-                send_near(side, line, o, 1 - o)
-        for o in range(2):
-            for side in sides:
-                send_near(side, line, o, o)
+    def send_back(o):
+        s = me.col_slab(0, 0)
+        part[1, s, o] = total(col, o).astype(BF16)
+        returned[o] = start(part.at[1, s, o], land_turn.at[o], 58 + o, me.back)
+
+    pl.when(off_diagonal)(lambda: spectra(((0, (0, 2)), (1, (1, 2))), me.way_in[0:2]))
+    for copy in row_far:
+        copy.wait_recv()
+    pl.when(on_diagonal)(lambda: spectra(((1, (0, 0)), (2, (0, 1))), me.way_in))
+    col_x[1][1].wait_recv()
+    col_far[1].append(pass_far(col, 1, 1))
+    for copy in col_far[0]:
+        copy.wait_recv()
+    pl.when(off_diagonal)(lambda: spectra(((0, (0, 2)), (1, (1, 2))), me.way_in[2:4]))
+    pl.when(on_diagonal)(lambda: spectra(((0, (k, 2)),), me.way_in, 2))
+    table.wait()
+    solve(2 + d)
+
+    def weigh(q):
+        terms = orb[q // 2, me.slab, q % 2, 0:16, 384:512].astype(F32)[0:8]
+        occupied[q] = jnp.broadcast_to(terms[:, 120:121] + terms[:, 121:122], (8, LANES))
+
+    for q in range(3):
+        weigh(q)
+
+    def first_off(slabs):
+        v = backward(w, gather, cas, [(s, p) for s in slabs for p in range(2)])
+        for n, s in enumerate(slabs):
+            v0, v1 = v[2 * n : 2 * n + 2]
+            acc[0, s] = weighed(2, s) * v0
+            acc[1, s] = weighed(2, s) * v1
+            acc[3, s] = jnp.zeros((ROWS, LANES), F32)
+            part[1, s, 0] = (weighed(0, s) * v0 + weighed(1, s) * v1).astype(BF16)
+
+    def first_on(slabs):
+        v = backward(w, gather, cas, [(s, p) for s in slabs for p in range(3)])
+        for n, s in enumerate(slabs):
+            v0, v1, v2 = v[3 * n : 3 * n + 3]
+            acc[0, s] = weighed(0, s) * v1 + weighed(1, s) * v2
+            acc[1, s] = weighed(0, s) * v2
+            acc[k, s] += weighed(2, s) * v0
+            acc[3, s] = jnp.zeros((ROWS, LANES), F32)
+            part[1, s, 0] = (weighed(k, s) * v0).astype(BF16)
+
+    def first(steps):
+        pl.when(off_diagonal)(lambda: over(steps, 1, first_off))
+        pl.when(on_diagonal)(lambda: over(steps, 1, first_on))
+
+    first(me.way_out[0:1])
+    send_far(col, 0)
+    first(me.way_out[1:4])
+    send_near(col, 0, 1)
+
+    def later(i, j, factor, steps, done):
+        def body(slabs):
+            for s, v in zip(slabs, backward(w, gather, cas, [(s, 0) for s in slabs])):
+                acc[i, s] += weighed(j, s) * v
+                acc[j, s] += weighed(i, s, factor) * v
+                for q in done:
+                    part[q // 2, s, q % 2] = acc[q, s].astype(BF16)
+
+        over(steps, 2, body)
+
+    col_own[1][1].wait_recv()
+    col_x[1][0].wait_recv()
+    for copy in col_far[1]:
+        copy.wait_recv()
+    weigh(3)
+    i, j = d * (1 - k), 3 - 2 * d * (1 - k)
+    factor = 1.0 - (d * (1 - k)).astype(F32)
+    spectra(((0, (i, j)),), (2, 1, 3, 0), 2)
+    solve(1)
+    send_near(col, 0, 0)
+    later(i, j, factor, (2, 1), (0,))
+    send_far(row, 0)
+    later(i, j, factor, (3, 0), (0,))
+    send_near(row, 0, 1)
+
+    j = 3 - 2 * d * k
+    factor = 1.0 - (d * k).astype(F32)
+    spectra(((0, (1, j)),), (2, 1, 3, 0), 2)
+    solve(1)
+    send_across(col, 0)
+    later(1, j, factor, me.way_out[0:2], (1, 3))
+    send_far(col, 1)
+    send_far(row, 1)
+    later(1, j, factor, me.way_out[2:4], (1, 3))
+    send_near(col, 1, 0)
+    send_near(row, 1, 0)
+    send_near(row, 0, 0)
+    send_back(0)
+    send_near(col, 1, 1)
+    send_near(row, 1, 1)
+    send_across(row, 0)
+    send_across(col, 1)
+    send_across(row, 1)
+    send_back(1)
     for o in range(2):
-        for side in sides:
-            send_across(side, o)
-    returned = []
-    for o in range(2):
-        part[1, me.col_slab(0, 0), o] = total(col, o).astype(BF16)
-        returned.append(start(part.at[1, me.col_slab(0, 0), o], land_turn.at[o], 58 + o, me.back))
-    for o in range(2):
-        field[o] = total(row, o)
+        acc[o, 0] = total(row, o)
     for o in range(2):
         returned[o].wait_recv()
-        whole = field[o] + land_turn[o].astype(F32)
+        whole = acc[o, 0] + land_turn[o].astype(F32)
         blocks = [whole[:, 72 * t : 72 * t + 72] for t in range(7)]
         for x in range(9):
             out[o, x] = lines_of(blocks, 72 * x, 72)
@@ -374,8 +443,8 @@
         out_specs=vmem,
         scratch_shapes=[
             pltpu.VMEM((2, 8, 2, *piece), BF16),
-            pltpu.VMEM((5, N * N, 128), F32),
-            pltpu.VMEM((4, *piece), F32),
+            pltpu.VMEM((3, N * N, 128), F32),
+            pltpu.VMEM((4, 8, *piece), F32),
             pltpu.VMEM((2, 8, 2, *piece), BF16),
             pltpu.VMEM((2, 2, 2, *piece), BF16),
             pltpu.VMEM((2, 2, 2, 2, *piece), BF16),

time: 81.4 us -> 75.2 us (0.924)
  the two profiles are of different devices: /device:TPU:35 before, /device:TPU:25 now
where the time goes in v2:
time: 75.2 us; the launch traced here: 74.6 us
  Pallas kernels  72.7 us (97%)
  local copies, waits for them, and re-layouts  1.97 us (3%)
    pallas_call x1, Pallas kernels, on_device(): pl.pallas_call(kernel, out_shape=jax.ShapeDtypeStruct(orbitals.shape, F32...  72.7 us
    unnamed x1, local copies, waits for them, and re-layouts  1.97 us

profile of v2, /device:TPU:25, one launch (start us, length us, event | category | flops | bytes accessed | tf_op | source)
XLA Modules:
  0.0 74.6 jit_solution(13626965535220318233)
XLA Ops:
  0.0 72.7 %exchange.1 = f32[2,9,72,72]{3,2,1,0:T(8,128)} custom-call(f32[2,9,72,72]{3,2,1,0:T(8,128)} %mine.1, f32[2]{0:T(128)} %occupation.1, bf16[4,256,256]{2,1,0:T(8,128)(2,1)} %constant.14.spread, bf16[72,72]{1,0:T(8,128)(2,1)} %constant.15.cas, bf16[4,256,256]{2,1,0:T(8,128)(2,1)} %constant.16.gather, f32[72,72,128]{2,1,0:T(8,128)} %constant.11.clone.coulomb_hbm), custom_call_target="tpu_custom_call" | custom-call | tf_op jit(solution)/shard_map/exchange/pallas_call | solution.py:439
  72.7 2.0 %copy.8 = f32[2,9,72,72]{3,2,1,0:T(8,128)} copy(f32[2,9,72,72]{3,2,1,0:T(8,128)} %exchange.1) | data formatting | bytes 746496

commit v3 on v2

--- a/solution.py
+++ b/solution.py
@@ -171,7 +171,8 @@
     me = Place()
     started = []
 
-    def start(source, target, index, device):
+    def start(source, target, device):
+        index = len(started)
         copy = pltpu.make_async_remote_copy(
             src_ref=source,
             dst_ref=target,
@@ -193,239 +194,215 @@
         orb[0, me.slab, o] = pack(mine[o], occupation[o])
     pl.semaphore_wait(barrier, len(me.partners()))
 
-    row = (0, 0, me.row_slab, me.row_x, me.row_ring)
-    col = (1, 14, me.col_slab, me.col_x, me.col_ring)
+    row = (0, me.row_slab, me.row_x, me.row_ring)
+    col = (1, me.col_slab, me.col_x, me.col_ring)
     sides = (col, row)
 
     def own(side, o):
-        ab, base, slab, x, ring = side
+        ab, slab, x, ring = side
         piece = orb.at[ab, slab(0, 0), o]
-        return [start(piece, piece, base + 3 * o + n, device) for n, device in enumerate((x, *ring))]
+        return [start(piece, piece, device) for device in (x, *ring)]
 
     def pass_x(side, o):
-        ab, base, slab, _, ring = side
+        ab, slab, _, ring = side
         piece = orb.at[ab, slab(0, 1), o]
-        return [start(piece, piece, base + 6 + 2 * o + n, ring[n]) for n in range(2)]
+        return [start(piece, piece, ring[n]) for n in range(2)]
 
     def pass_far(side, line, n):
-        ab, base, slab, _, ring = side
+        ab, slab, _, ring = side
         piece = orb.at[ab, slab((3, 1)[n], line), n]
-        return start(piece, piece, base + 10 + 2 * line + n, ring[n])
-
-    turned = [start(orb.at[0, me.slab, o], orb.at[1, me.slab, o], 28 + o, me.turn) for o in range(2)]
+        return start(piece, piece, ring[n])
+
+    def slab_at(steps, t):
+        step = steps[0]
+        for n in range(1, len(steps)):
+            reached = (t // 2 + 4 - n) // 4
+            step = step + (steps[n] - steps[n - 1]) * reached
+        return 2 * ((me.z + step) % 4) + t % 2
+
+    k = me.k
+    on_diagonal, off_diagonal = me.diagonal == 1, me.diagonal == 0
+    block = tuple((p, (p // 2, 2 + p % 2)) for p in range(4))
+
+    def spectra(pairs, steps):
+        def body(t, _):
+            s = slab_at(steps, t)
+            forward(orb, w, spread, cas, [(i, j, s, p) for p, (i, j) in pairs])
+            return 0
+
+        lax.fori_loop(0, 2 * len(steps), body, 0)
+
+    def solve(first, count):
+        def body(t, _):
+            middle(w, cas, coulomb, first + t // (N // BLOCK), t % (N // BLOCK) * BLOCK)
+            return 0
+
+        lax.fori_loop(0, count * (N // BLOCK), body, 0)
+
+    inner = ((2, (0, 0)), (3, (0, 1)), (4, (1, 1)))
+
+    def inner_spectra(step):
+        pl.when(on_diagonal)(lambda: spectra(inner, (step,)))
+
+    turned = [start(orb.at[0, me.slab, o], orb.at[1, me.slab, o], me.turn) for o in range(2)]
     row_own = [own(row, o) for o in range(2)]
-    row_x, col_x, col_own, row_far, col_far = [], [], [], [], [[], []]
+    row_x, col_x, col_own, far = [], [], [], []
     for o in range(2):
         row_own[o][0].wait_recv()
         row_x.append(pass_x(row, o))
     turned[0].wait_recv()
     col_own.append(own(col, 0))
     row_own[0][1].wait_recv()
-    row_far.append(pass_far(row, 0, 0))
+    far.append(pass_far(row, 0, 0))
     turned[1].wait_recv()
     col_own.append(own(col, 1))
     row_own[1][2].wait_recv()
-    row_far.append(pass_far(row, 0, 1))
-    col_own[0][0].wait_recv()
-    col_x.append(pass_x(col, 0))
-    col_own[0][1].wait_recv()
-    col_far[0].append(pass_far(col, 0, 0))
+    far.append(pass_far(row, 0, 1))
+    inner_spectra(0)
+    for o in range(2):
+        col_own[o][0].wait_recv()
+        col_x.append(pass_x(col, o))
     for n in range(2):
         row_x[n][n].wait_recv()
-        row_far.append(pass_far(row, 1, n))
-    col_own[1][0].wait_recv()
-    col_x.append(pass_x(col, 1))
-    col_x[0][0].wait_recv()
-    col_far[0].append(pass_far(col, 1, 0))
-    col_own[1][2].wait_recv()
-    col_far[1].append(pass_far(col, 0, 1))
+        far.append(pass_far(row, 1, n))
     for n in range(2):
         row_own[n][2 - n].wait_recv()
         row_x[n][1 - n].wait_recv()
-    col_own[0][2].wait_recv()
-    col_x[0][1].wait_recv()
-
-    k, d = me.k, me.diagonal
-    on_diagonal, off_diagonal = d == 1, d == 0
-
-    def step_at(steps, t):
-        step = steps[0]
-        for n in range(1, len(steps)):
-            step = step + (steps[n] - steps[n - 1]) * ((t + len(steps) - n) // len(steps))
-        return step
-
-    def slabs_at(step):
-        return [2 * ((me.z + step) % 4) + line for line in range(2)]
-
-    def over(steps, group, body):
-        firsts = [steps[n::group] for n in range(group)]
-
-        def run(t, _):
-            body([slab for own_steps in firsts for slab in slabs_at(step_at(own_steps, t))])
+    inner_spectra(1)
+    for n in range(2):
+        col_own[n][1 + n].wait_recv()
+        far.append(pass_far(col, 0, n))
+    inner_spectra(3)
+    for n in range(2):
+        col_x[n][n].wait_recv()
+        far.append(pass_far(col, 1, n))
+    for copy in far[:4]:
+        copy.wait_recv()
+    table.wait()
+    inner_spectra(2)
+    pl.when(on_diagonal)(lambda: solve(2, 3))
+    for n in range(2):
+        col_own[n][2 - n].wait_recv()
+        col_x[n][1 - n].wait_recv()
+    across_pairs = ((0, (0, 2 + k)), (1, (1, 3 - k)))
+    pl.when(on_diagonal)(lambda: spectra(across_pairs, me.way_in[0:2]))
+    pl.when(off_diagonal)(lambda: spectra(block, me.way_in[0:2]))
+    for copy in far[4:]:
+        copy.wait_recv()
+    pl.when(off_diagonal)(lambda: spectra(block, me.way_in[2:4]))
+    pl.when(on_diagonal)(lambda: spectra(across_pairs, me.way_in[2:4]))
+
+    for q in range(4):
+        terms = orb[q // 2, me.slab, q % 2, 0:16, 384:512].astype(F32)[0:8]
+        occupied[q] = jnp.broadcast_to(terms[:, 120:121] + terms[:, 121:122], (8, LANES))
+    solve(0, 4 - 2 * me.diagonal)
+
+    def weighed(q, s):
+        return orb[q // 2, s, q % 2].astype(F32) * occupied[q, 0:1, :]
+
+    def block_fields(s):
+        v = backward(w, gather, cas, [(s, p) for p in range(4)])
+        for o in range(2):
+            part[0, s, o] = (weighed(2, s) * v[2 * o] + weighed(3, s) * v[2 * o + 1]).astype(BF16)
+            part[1, s, o] = (weighed(0, s) * v[o] + weighed(1, s) * v[2 + o]).astype(BF16)
+
+    def diagonal_fields(s):
+        v = backward(w, gather, cas, [(s, p) for p in range(5)])
+        part[0, s, 0] = (weighed(0, s) * v[2] + weighed(1, s) * v[3] + weighed(2 + k, s) * v[0]).astype(BF16)
+        part[0, s, 1] = (weighed(0, s) * v[3] + weighed(1, s) * v[4] + weighed(3 - k, s) * v[1]).astype(BF16)
+        part[1, s, k] = (weighed(0, s) * v[0]).astype(BF16)
+        part[1, s, 1 - k] = (weighed(1, s) * v[1]).astype(BF16)
+
+    def fields(steps):
+        def body(t, _):
+            s = slab_at(steps, t)
+            pl.when(off_diagonal)(lambda: block_fields(s))
+            pl.when(on_diagonal)(lambda: diagonal_fields(s))
             return 0
 
-        lax.fori_loop(0, len(steps) // group, run, 0)
-
-    def spectra(pairs, steps, group=1):
-        over(
-            steps,
-            group,
-            lambda slabs: forward(
-                orb, w, spread, cas, [(i, j, s, p) for s in slabs for p, (i, j) in pairs]
-            ),
-        )
-
-    def solve(count):
-        def body(t, _):
-            middle(w, cas, coulomb, t // (N // BLOCK), t % (N // BLOCK) * BLOCK)
-            return 0
-
-        lax.fori_loop(0, count * (N // BLOCK), body, 0)
-
-    def weighed(q, s, factor=None):
-        weight = occupied[q, 0:1, :]
-        if factor is not None:
-            weight = weight * factor
-        return orb[q // 2, s, q % 2].astype(F32) * weight
+        lax.fori_loop(0, 2 * len(steps), body, 0)
 
     def add(*values):
         return sum((value.astype(F32) for value in values[1:]), values[0].astype(F32))
 
+    half = (slice(0, ROWS // 2), slice(ROWS // 2, ROWS))
     far, near, across, returned = {}, {}, {}, {}
 
     def send_far(side, o):
-        ab, base, slab, _, ring = side
+        ab, slab, _, ring = side
         for line in (1, 0):
-            source = part.at[ab, slab(2, line), o]
-            far[ab, line, o] = start(source, land_half.at[ab, o, line], 30 + base + 2 * line + o, ring[o])
-
-    def send_near(side, o, n):
-        ab, base, slab, _, ring = side
-        for line in (1, 0):
+            for h in range(2):
+                source = part.at[ab, slab(2, line), o, half[h]]
+                far[ab, line, o, h] = start(source, land_half.at[ab, o, line, h], ring[h])
+
+    def send_near(side, o, line, passing):
+        ab, slab, _, ring = side
+        for h in range(2):
+            n = h if passing else 1 - h
             s = slab((1, 3)[n], line)
-            if o == n:
-                far[ab, line, n].wait_recv()
-                part[ab, s, o] = add(part[ab, s, o], land_half[ab, n, line]).astype(BF16)
-            index = 34 + base + 4 * line + 2 * o + n
-            near[ab, line, o, n] = start(part.at[ab, s, o], land_ring.at[ab, n, line, o], index, ring[n])
+            if passing:
+                far[ab, line, o, h].wait_recv()
+                part[ab, s, o, half[h]] = add(part[ab, s, o, half[h]], land_half[ab, o, line, h]).astype(BF16)
+            source, target = part.at[ab, s, o, half[h]], land_ring.at[ab, n, line, o, half[h]]
+            near[ab, line, o, h, n] = start(source, target, ring[n])
 
     def send_across(side, o):
-        ab, base, slab, x, _ = side
+        ab, slab, x, _ = side
         s = slab(0, 1)
+        for h in range(2):
+            for n in range(2):
+                near[ab, 1, o, h, n].wait_recv()
+            landed = [land_ring[ab, n, 1, o, half[h]] for n in range(2)]
+            part[ab, s, o, half[h]] = add(part[ab, s, o, half[h]], *landed).astype(BF16)
+            across[ab, o, h] = start(part.at[ab, s, o, half[h]], land_x.at[ab, o, half[h]], x)
+
+    def total(side, o, h):
+        ab, slab, _, _ = side
         for n in range(2):
-            near[ab, 1, o, n].wait_recv()
-        part[ab, s, o] = add(part[ab, s, o], land_ring[ab, 0, 1, o], land_ring[ab, 1, 1, o]).astype(BF16)
-        across[ab, o] = start(part.at[ab, s, o], land_x.at[ab, o], 42 + base + o, x)
-
-    def total(side, o):
-        ab, _, slab, _, _ = side
-        for n in range(2):
-            near[ab, 0, o, n].wait_recv()
-        across[ab, o].wait_recv()
-        return add(part[ab, slab(0, 0), o], land_ring[ab, 0, 0, o], land_ring[ab, 1, 0, o], land_x[ab, o])
+            near[ab, 0, o, h, n].wait_recv()
+        across[ab, o, h].wait_recv()
+        landed = [land_ring[ab, n, 0, o, half[h]] for n in range(2)]
+        return add(part[ab, slab(0, 0), o, half[h]], *landed, land_x[ab, o, half[h]])
 
     def send_back(o):
         s = me.col_slab(0, 0)
-        part[1, s, o] = total(col, o).astype(BF16)
-        returned[o] = start(part.at[1, s, o], land_turn.at[o], 58 + o, me.back)
-
-    pl.when(off_diagonal)(lambda: spectra(((0, (0, 2)), (1, (1, 2))), me.way_in[0:2]))
-    for copy in row_far:
-        copy.wait_recv()
-    pl.when(on_diagonal)(lambda: spectra(((1, (0, 0)), (2, (0, 1))), me.way_in))
-    col_x[1][1].wait_recv()
-    col_far[1].append(pass_far(col, 1, 1))
-    for copy in col_far[0]:
-        copy.wait_recv()
-    pl.when(off_diagonal)(lambda: spectra(((0, (0, 2)), (1, (1, 2))), me.way_in[2:4]))
-    pl.when(on_diagonal)(lambda: spectra(((0, (k, 2)),), me.way_in, 2))
-    table.wait()
-    solve(2 + d)
-
-    def weigh(q):
-        terms = orb[q // 2, me.slab, q % 2, 0:16, 384:512].astype(F32)[0:8]
-        occupied[q] = jnp.broadcast_to(terms[:, 120:121] + terms[:, 121:122], (8, LANES))
-
-    for q in range(3):
-        weigh(q)
-
-    def first_off(slabs):
-        v = backward(w, gather, cas, [(s, p) for s in slabs for p in range(2)])
-        for n, s in enumerate(slabs):
-            v0, v1 = v[2 * n : 2 * n + 2]
-            acc[0, s] = weighed(2, s) * v0
-            acc[1, s] = weighed(2, s) * v1
-            acc[3, s] = jnp.zeros((ROWS, LANES), F32)
-            part[1, s, 0] = (weighed(0, s) * v0 + weighed(1, s) * v1).astype(BF16)
-
-    def first_on(slabs):
-        v = backward(w, gather, cas, [(s, p) for s in slabs for p in range(3)])
-        for n, s in enumerate(slabs):
-            v0, v1, v2 = v[3 * n : 3 * n + 3]
-            acc[0, s] = weighed(0, s) * v1 + weighed(1, s) * v2
-            acc[1, s] = weighed(0, s) * v2
-            acc[k, s] += weighed(2, s) * v0
-            acc[3, s] = jnp.zeros((ROWS, LANES), F32)
-            part[1, s, 0] = (weighed(k, s) * v0).astype(BF16)
-
-    def first(steps):
-        pl.when(off_diagonal)(lambda: over(steps, 1, first_off))
-        pl.when(on_diagonal)(lambda: over(steps, 1, first_on))
-
-    first(me.way_out[0:1])
+        for h in range(2):
+            part[1, s, o, half[h]] = total(col, o, h).astype(BF16)
+            returned[o, h] = start(part.at[1, s, o, half[h]], land_turn.at[o, half[h]], me.back)
+
+    fields(me.way_out[0:1])
     send_far(col, 0)
-    first(me.way_out[1:4])
-    send_near(col, 0, 1)
-
-    def later(i, j, factor, steps, done):
-        def body(slabs):
-            for s, v in zip(slabs, backward(w, gather, cas, [(s, 0) for s in slabs])):
-                acc[i, s] += weighed(j, s) * v
-                acc[j, s] += weighed(i, s, factor) * v
-                for q in done:
-                    part[q // 2, s, q % 2] = acc[q, s].astype(BF16)
-
-        over(steps, 2, body)
-
-    col_own[1][1].wait_recv()
-    col_x[1][0].wait_recv()
-    for copy in col_far[1]:
-        copy.wait_recv()
-    weigh(3)
-    i, j = d * (1 - k), 3 - 2 * d * (1 - k)
-    factor = 1.0 - (d * (1 - k)).astype(F32)
-    spectra(((0, (i, j)),), (2, 1, 3, 0), 2)
-    solve(1)
-    send_near(col, 0, 0)
-    later(i, j, factor, (2, 1), (0,))
+    send_far(col, 1)
+    fields(me.way_out[1:2])
     send_far(row, 0)
-    later(i, j, factor, (3, 0), (0,))
-    send_near(row, 0, 1)
-
-    j = 3 - 2 * d * k
-    factor = 1.0 - (d * k).astype(F32)
-    spectra(((0, (1, j)),), (2, 1, 3, 0), 2)
-    solve(1)
+    send_far(row, 1)
+    fields(me.way_out[2:4])
+    for side in sides:
+        send_near(side, 0, 1, False)
+    for side in sides:
+        send_near(side, 0, 0, False)
+    for line in (1, 0):
+        for side in sides:
+            send_near(side, 0, line, True)
+    for line in (1, 0):
+        for side in sides:
+            send_near(side, 1, line, False)
+    for line in (1, 0):
+        for side in sides:
+            send_near(side, 1, line, True)
     send_across(col, 0)
-    later(1, j, factor, me.way_out[0:2], (1, 3))
-    send_far(col, 1)
-    send_far(row, 1)
-    later(1, j, factor, me.way_out[2:4], (1, 3))
-    send_near(col, 1, 0)
-    send_near(row, 1, 0)
-    send_near(row, 0, 0)
+    send_across(row, 0)
     send_back(0)
-    send_near(col, 1, 1)
-    send_near(row, 1, 1)
-    send_across(row, 0)
     send_across(col, 1)
     send_across(row, 1)
     send_back(1)
     for o in range(2):
-        acc[o, 0] = total(row, o)
+        for h in range(2):
+            acc[o, half[h]] = total(row, o, h)
     for o in range(2):
-        returned[o].wait_recv()
-        whole = acc[o, 0] + land_turn[o].astype(F32)
+        for h in range(2):
+            returned[o, h].wait_recv()
+        whole = acc[o] + land_turn[o].astype(F32)
         blocks = [whole[:, 72 * t : 72 * t + 72] for t in range(7)]
         for x in range(9):
             out[o, x] = lines_of(blocks, 72 * x, 72)
@@ -443,17 +420,17 @@
         out_specs=vmem,
         scratch_shapes=[
             pltpu.VMEM((2, 8, 2, *piece), BF16),
-            pltpu.VMEM((3, N * N, 128), F32),
-            pltpu.VMEM((4, 8, *piece), F32),
+            pltpu.VMEM((5, N * N, 128), F32),
+            pltpu.VMEM((2, *piece), F32),
             pltpu.VMEM((2, 8, 2, *piece), BF16),
-            pltpu.VMEM((2, 2, 2, *piece), BF16),
+            pltpu.VMEM((2, 2, 2, 2, ROWS // 2, LANES), BF16),
             pltpu.VMEM((2, 2, 2, 2, *piece), BF16),
             pltpu.VMEM((2, 2, *piece), BF16),
             pltpu.VMEM((2, *piece), BF16),
             pltpu.VMEM((N, N, 128), F32),
             pltpu.VMEM((4, 8, LANES), F32),
-            pltpu.SemaphoreType.DMA((60,)),
-            pltpu.SemaphoreType.DMA((60,)),
+            pltpu.SemaphoreType.DMA((90,)),
+            pltpu.SemaphoreType.DMA((90,)),
             pltpu.SemaphoreType.DMA,
         ],
         compiler_params=pltpu.CompilerParams(

time: 75.2 us -> 70.9 us (0.943)
  the two profiles are of different devices: /device:TPU:25 before, /device:TPU:1 now
where the time goes in v3:
time: 70.9 us; the launch traced here: 70.7 us
  Pallas kernels  68.8 us (97%)
  local copies, waits for them, and re-layouts  1.97 us (3%)
    pallas_call x1, Pallas kernels, on_device(): pl.pallas_call(kernel, out_shape=jax.ShapeDtypeStruct(orbitals.shape, F32...  68.8 us
    unnamed x1, local copies, waits for them, and re-layouts  1.97 us

profile of v3, /device:TPU:1, one launch (start us, length us, event | category | flops | bytes accessed | tf_op | source)
XLA Modules:
  0.0 70.7 jit_solution(3376633138704603203)
XLA Ops:
  0.0 68.8 %exchange.1 = f32[2,9,72,72]{3,2,1,0:T(8,128)} custom-call(f32[2,9,72,72]{3,2,1,0:T(8,128)} %mine.1, f32[2]{0:T(128)} %occupation.1, bf16[4,256,256]{2,1,0:T(8,128)(2,1)} %constant.14.spread, bf16[72,72]{1,0:T(8,128)(2,1)} %constant.15.cas, bf16[4,256,256]{2,1,0:T(8,128)(2,1)} %constant.16.gather, f32[72,72,128]{2,1,0:T(8,128)} %constant.11.clone.coulomb_hbm), custom_call_target="tpu_custom_call" | custom-call | tf_op jit(solution)/shard_map/exchange/pallas_call | solution.py:416
  68.8 2.0 %copy.8 = f32[2,9,72,72]{3,2,1,0:T(8,128)} copy(f32[2,9,72,72]{3,2,1,0:T(8,128)} %exchange.1) | data formatting | bytes 746496
